TPU v7x, 32 devices: a whole 2x2x4 slice. The times are simulated.
32 devices in a mesh: parts: 2 (over x), aux: 16 (over z, y, core).
Axes of the slice: x: 2, y: 2, z: 4, core: 2. Of those that a mesh axis runs over, the one named last changes fastest.
Arguments:
- tiles: bfloat16 [32, 8, 8, 128, 128], P(('parts', 'aux')), parts along dimension 0, may hold values from -6 to 6
- mu_list: int32 [32, 8], P(('parts', 'aux')), parts along dimension 0, may hold values from 0 to 7
- lam_list: int32 [32, 8], P(('parts', 'aux')), parts along dimension 0, may hold values from 0 to 7
- tile_count: int32 [32], P(('parts', 'aux')), parts along dimension 0, may hold values from 1 to 8, as said below
- coeff: bfloat16 [2048, 256], P(('parts', 'aux')), parts along dimension 0, may hold values from -0.5 to 0.5
- owner: int32 [32], P('parts'), parts along dimension 0, may hold values from 0 to 15, each once
Outputs:
- exchange: float32 [2048, 1024], P(('parts', 'aux')), parts along dimension 0
There are 2 independent parts, one for each index of `parts`. A program takes and returns all parts, laid end to end along the dimension named above; each array names one. Nothing has to cross between parts.
Inputs may be any that keep to these rules, and one draw needn't show every extreme that they name: Slots from tile_count on are padding and are ignored; in every draw some shard uses all 8 slots.
All inputs are finite; a program needn't handle non-finite values.
Results may differ from a plain program's by a relative error of at most 0.00088.
Values may be sent and summed in bfloat16 or wider, within the bound.
A program may use at most 64 MiB of HBM per device.

v0:
```python
import jax
import jax.numpy as jnp
from jax import lax
from jax.sharding import PartitionSpec as P


def body(tiles, mu_list, lam_list, tile_count, coeff, owner):
    shards = lax.axis_size("aux")
    whole_coeff = lax.all_gather(coeff, "aux", axis=0, tiled=True)
    nbasis, occupied = whole_coeff.shape
    slots = tiles.shape[1]
    aux_local = tiles.shape[2]
    block = tiles.shape[3]
    nblocks = nbasis // block
    tile_rows = nbasis // shards
    picked = whole_coeff.reshape(nblocks, block, occupied)[lam_list[0]]
    live = (jnp.arange(slots) < tile_count[0]).astype(jnp.float32)
    products = jnp.einsum("tpml,tlo->tpmo", tiles[0], picked, preferred_element_type=jnp.float32)
    placing = (mu_list[0][:, None] == jnp.arange(nblocks)[None, :]).astype(jnp.float32) * live[
        :, None
    ]
    half_form = jnp.einsum(
        "tb,tpmo->pbmo", placing, products, precision=lax.Precision.HIGHEST
    ).astype(jnp.bfloat16)
    ordered = half_form.reshape(aux_local, shards, tile_rows, occupied)[:, owner].reshape(
        aux_local, nbasis, occupied
    )
    scale = 1.0 / (aux_local * shards * occupied)
    summed = lax.psum_scatter(
        jnp.einsum("prk,psk->rs", ordered, ordered, preferred_element_type=jnp.float32),
        "aux",
        scatter_dimension=0,
        tiled=True,
    )
    return summed * scale


def solution(mesh):
    return jax.shard_map(
        body,
        mesh=mesh,
        in_specs=(
            P(("parts", "aux"), None, None, None, None),
            P(("parts", "aux"), None),
            P(("parts", "aux"), None),
            P(("parts", "aux")),
            P(("parts", "aux"), None),
            P("parts"),
        ),
        out_specs=P(("parts", "aux"), None),
        check_vma=False,
    )
```

profile of v0, /device:TPU:0, one launch (start us, length us, event | category | flops | bytes accessed | tf_op | source)
XLA Modules:
  0.0 151.5 jit_solution(12048981923072878204)
XLA Ops:
  6.5 0.0 copy-start
  6.5 0.0 reduce-scatter.2.cloned.1.call-start
  6.5 24.9 %all_gather.3 = bf16[1024,256]{1,0:T(8,128)(2,1)S(1)} all-gather(bf16[64,256]{1,0:T(8,128)(2,1)} %param.10), channel_id=1, replica_groups=mesh['parts'=2,'aux'=16] {'aux'}, dimensions={0}, use_global_device_ids=true | all-gather | bytes 557056 | tf_op jit(solution)/shard_map/all_gather | solution.py:9
  31.4 0.7 fusion.7
  32.1 0.6 gather_fusion
  32.7 0.0 copy-done
  32.7 4.5 %convolution_bitcast_fusion = f32[8,8,128,256]{2,3,1,0:T(8,128)} fusion(bf16[1,8,8,128,128]{4,3,2,1,0:T(8,128)(2,1)S(1)} %copy-done, bf16[8,128,256]{2,1,0:T(8,128)(2,1)S(1)} %gather_fusion), kind=kOutput, calls=%fused_computation.3 | convolution fusion | flops 536870912 | bytes 11010048 | tf_op jit(solution)/shard_map/tpml,tlo->tpmo/dot_general | solution.py:18
  37.2 0.0 copy-start.1
  37.2 9.2 %copy.12 = f32[8,8,128,256]{3,0,2,1:T(8,128)} copy(f32[8,8,128,256]{2,3,1,0:T(8,128)} %convolution_bitcast_fusion) | data formatting | bytes 16777216 | tf_op jit(solution)/shard_map/tpml,tlo->tpmo/dot_general | solution.py:18
  47.1 0.0 copy-done.1
  47.1 9.4 %convert_bitcast_fusion = bf16[8,8,128,256]{3,1,2,0:T(8,128)(2,1)S(1)} fusion(f32[8,8,128,256]{3,0,2,1:T(8,128)} %copy.12, f32[8]{0:T(128)S(1)} %compare_convert_fusion, s32[8]{0:T(128)S(1)} %bitcast.37), kind=kOutput, calls=%fused_computation.2 | convolution fusion | flops 203423872 | bytes 12582976 | tf_op jit(solution)/shard_map/tb,tpmo->pbmo/dot_general | solution.py:22
  56.6 0.0 copy-start.2
  56.6 3.0 %copy.13 = bf16[8,8,128,256]{3,2,1,0:T(8,128)(2,1)} copy(bf16[8,8,128,256]{3,1,2,0:T(8,128)(2,1)S(1)} %convert_bitcast_fusion) | data formatting | bytes 8388608 | tf_op jit(solution)/shard_map/convert_element_type | solution.py:24
  59.6 0.0 copy-done.2
  59.6 5.0 %gather_fusion.1 = bf16[16,8,64,256]{3,2,1,0:T(8,128)(2,1)} fusion(bf16[8,16,64,256]{3,2,1,0:T(8,128)(2,1)} %bitcast.33, s32[1024]{0:T(1024)S(1)} %pad_clamp_fusion), kind=kCustom, calls=%fused_computation.1 | custom fusion | bytes 8388672 | tf_op jit(solution)/shard_map/gather | solution.py:25
  64.6 2.5 %copy.14 = bf16[8,16,64,256]{3,2,1,0:T(8,128)(2,1)S(1)} copy(bf16[8,16,64,256]{3,2,0,1:T(8,128)(2,1)} %bitcast.34) | data formatting | bytes 8388608 | tf_op jit(solution)/shard_map/gather | solution.py:25
  67.1 6.1 %convolution_bitcast_fusion.1 = f32[1024,1024]{1,0:T(8,128)} fusion(bf16[8,1024,256]{2,1,0:T(8,128)(2,1)S(1)} %bitcast.35), kind=kOutput, calls=%fused_computation.4 | convolution fusion | flops 4294967296 | bytes 8388608 | tf_op jit(solution)/shard_map/prk,psk->rs/dot_general | solution.py:30
  73.2 0.0 reduce-scatter.2.cloned.1.call-update
  73.2 69.8 %reduce-scatter.2.cloned.1.call-done = f32[64,1024]{1,0:T(8,128)} async-done(((f32[1024,1024]{1,0:T(8,128)}), f32[64,1024]{1,0:T(8,128)}) %reduce-scatter.2.cloned.1.call-update) | async-done | bytes 262160 | tf_op jit(solution)/shard_map/reduce_scatter | solution.py:29
  143.0 1.7 %broadcast_multiply_fusion = f32[64,1024]{1,0:T(8,128)} fusion(f32[64,1024]{1,0:T(8,128)} %reduce-scatter.2.cloned.1.call-done), kind=kLoop, calls=%fused_computation.7 | loop fusion | flops 65536 | bytes 524288 | tf_op jit(solution)/shard_map/mul | solution.py:35
  (4 shorter events, 0.0 us)
Async XLA Ops:
  6.5 26.2 %copy-start = (bf16[1,8,8,128,128]{4,3,2,1,0:T(8,128)(2,1)S(1)}, bf16[1,8,8,128,128]{4,3,2,1,0:T(8,128)(2,1)}, u32[]{:S(2)}) copy-start(bf16[1,8,8,128,128]{4,3,2,1,0:T(8,128)(2,1)} %param.6) | copy-start | bytes 6291460
  6.5 136.5 %reduce-scatter.2.cloned.1.call-start = ((), (), s32[]{:S(2)}) async-start(), calls=%async_computation.1 | async-start | bytes 4456448 | tf_op jit(solution)/shard_map/reduce_scatter | solution.py:29
  37.2 9.9 %copy-start.1 = (s32[1,8]{1,0:T(1,128)S(1)}, s32[1,8]{1,0:T(1,128)}, u32[]{:S(2)}) copy-start(s32[1,8]{1,0:T(1,128)} %param.7) | copy-start | bytes 100
  56.6 3.0 %copy-start.2 = (s32[16]{0:T(128)S(1)}, s32[16]{0:T(128)}, u32[]{:S(2)}) copy-start(s32[16]{0:T(128)} %param.11) | copy-start | bytes 196
Sparse Core Ops, SparseCore 0:
  73.3 69.6 reduce-scatter.1
where the time goes:
time: 152 us
  waiting for transfers between devices  69.8 us (46%)
  blocking collectives  24.9 us (16%)
  local copies, waits for them, and re-layouts  20.3 us (13%)
  matrix products  20.1 us (13%)
  between operations  14.1 us (9%)
  other arithmetic  2.35 us (2%)
    reduce_scatter x1, waiting for transfers between devices, body(): lax.psum_scatter(jnp.einsum('prk,psk->rs', ordered, ordered, preferred_el...  69.8 us
    all_gather x1, blocking collectives, body(): whole_coeff = lax.all_gather(coeff, 'aux', axis=0, tiled=True)  24.9 us
    dot_general x1, matrix products, body(): jnp.einsum('tb,tpmo->pbmo', placing, products, precision=lax.Precision.HI...  9.44 us
    dot_general x1, local copies, waits for them, and re-layouts, body(): jnp.einsum('tpml,tlo->tpmo', tiles[0], picked, preferred_element_type=jnp...  9.21 us
    gather x2, local copies, waits for them, and re-layouts, body(): half_form.reshape(aux_local, shards, tile_rows, occupied)[:, owner]  7.47 us
    dot_general x1, matrix products, body(): jnp.einsum('prk,psk->rs', ordered, ordered, preferred_element_type=jnp.fl...  6.09 us
    dot_general x1, matrix products, body(): jnp.einsum('tpml,tlo->tpmo', tiles[0], picked, preferred_element_type=jnp...  4.52 us
  transfers between devices with their start and end apart: 1, of which 1 were waited for; matrix products, arithmetic and copies ran while one was open for 0% of the time, Pallas kernels for 0%

commit v1 on v0

--- a/solution.py
+++ b/solution.py
@@ -6,7 +6,9 @@
 
 def body(tiles, mu_list, lam_list, tile_count, coeff, owner):
     shards = lax.axis_size("aux")
-    whole_coeff = lax.all_gather(coeff, "aux", axis=0, tiled=True)
+    whole_coeff = jnp.concatenate(
+        lax.all_to_all(jnp.stack([coeff] * lax.axis_size("aux")), "aux", 0, 0), axis=0
+    )
     nbasis, occupied = whole_coeff.shape
     slots = tiles.shape[1]
     aux_local = tiles.shape[2]

time: 152 us -> 152 us (level)
  blocking collectives: 24.9 us -> 0 us
  waiting for transfers between devices: 69.8 us -> 84.7 us
  starting transfers between devices: 0.01 us -> 7.43 us
  local copies, waits for them, and re-layouts: 20.3 us -> 22 us
    all_gather x1 -> x0, blocking collectives: 24.9 us -> none  [body(): whole_coeff = lax.all_gather(coeff, 'aux', axis=0, tiled=True)]
    all_to_all x0 -> x1, waiting for transfers between devices: none -> 12.4 us  [body(): lax.all_to_all(jnp.stack([coeff] * lax.axis_size('aux')), 'aux', 0, 0)]
    all_to_all x0 -> x1, starting transfers between devices: none -> 7.39 us  [body(): lax.all_to_all(jnp.stack([coeff] * lax.axis_size('aux')), 'aux', 0, 0)]
    reduce_scatter x1, waiting for transfers between devices: 69.8 us -> 72.3 us  [body(): lax.psum_scatter(jnp.einsum('prk,psk->rs', ordered, ordered, preferred_el...]
    another operation x0 -> x1, local copies, waits for them, and re-layouts: none -> 1.75 us  [body(): jnp.stack([coeff] * lax.axis_size('aux'))]
  transfers between devices with their start and end apart: 1 -> 2, of which waited for: 1 -> 2; matrix products, arithmetic and copies ran while one was open for 0% -> 1% of each run, Pallas kernels for 0% -> 0%
where the time goes in v1:
time: 152 us; the launch traced here: 151 us
  waiting for transfers between devices  84.7 us (56%)
  local copies, waits for them, and re-layouts  22 us (14%)
  matrix products  20 us (13%)
  between operations  14.1 us (9%)
  starting transfers between devices  7.43 us (5%)
  other arithmetic  3.01 us (2%)
    reduce_scatter x1, waiting for transfers between devices, body(): lax.psum_scatter(jnp.einsum('prk,psk->rs', ordered, ordered, preferred_el...  72.3 us
    all_to_all x1, waiting for transfers between devices, body(): lax.all_to_all(jnp.stack([coeff] * lax.axis_size('aux')), 'aux', 0, 0)  12.4 us
    dot_general x1, matrix products, body(): jnp.einsum('tb,tpmo->pbmo', placing, products, precision=lax.Precision.HI...  9.43 us
    dot_general x1, local copies, waits for them, and re-layouts, body(): jnp.einsum('tpml,tlo->tpmo', tiles[0], picked, preferred_element_type=jnp...  9.21 us
    gather x2, local copies, waits for them, and re-layouts, body(): half_form.reshape(aux_local, shards, tile_rows, occupied)[:, owner]  7.46 us
    all_to_all x1, starting transfers between devices, body(): lax.all_to_all(jnp.stack([coeff] * lax.axis_size('aux')), 'aux', 0, 0)  7.39 us
    dot_general x1, matrix products, body(): jnp.einsum('prk,psk->rs', ordered, ordered, preferred_element_type=jnp.fl...  6.08 us
    dot_general x1, matrix products, body(): jnp.einsum('tpml,tlo->tpmo', tiles[0], picked, preferred_element_type=jnp...  4.51 us
  transfers between devices with their start and end apart: 2, of which 2 were waited for; matrix products, arithmetic and copies ran while one was open for 1% of the time, Pallas kernels for 0%

profile of v1, /device:TPU:0, one launch (start us, length us, event | category | flops | bytes accessed | tf_op | source)
XLA Modules:
  0.0 151.3 jit_solution(17203938971172059097)
XLA Ops:
  6.5 0.0 copy-start
  6.5 1.8 %stack.2 = bf16[16,64,256]{2,1,0:T(8,128)(2,1)} broadcast(bf16[64,256]{1,0:T(8,128)(2,1)} %param.10), dimensions={1,2} | broadcast | bytes 557056 | tf_op jit(solution)/shard_map/stack | solution.py:10
  8.3 7.4 %all-to-all-start = ((bf16[16,64,256]{2,1,0:T(8,128)(2,1)}), bf16[16,64,256]{2,1,0:T(8,128)(2,1)S(1)}, u32[]{:S(2)}, u32[]{:S(2)}) async-start(bf16[16,64,256]{2,1,0:T(8,128)(2,1)} %stack.2), calls=%async_computation | async-start | bytes 1048576 | tf_op jit(solution)/shard_map/all_to_all | solution.py:10
  15.7 0.0 reduce-scatter.2.cloned.1.call-start
  16.4 0.7 fusion.7
  17.1 0.7 compare_select_fusion
  17.7 12.4 %all-to-all-done = bf16[16,64,256]{2,1,0:T(8,128)(2,1)S(1)} async-done(((bf16[16,64,256]{2,1,0:T(8,128)(2,1)}), bf16[16,64,256]{2,1,0:T(8,128)(2,1)S(1)}, u32[]{:S(2)}, u32[]{:S(2)}) %all-to-all-start) | async-done | bytes 524320 | tf_op jit(solution)/shard_map/all_to_all | solution.py:10
  30.2 0.6 gather_fusion
  30.7 0.0 copy-done
  30.8 4.5 %convolution_bitcast_fusion = f32[8,8,128,256]{2,3,1,0:T(8,128)} fusion(bf16[1,8,8,128,128]{4,3,2,1,0:T(8,128)(2,1)S(1)} %copy-done, bf16[8,128,256]{2,1,0:T(8,128)(2,1)S(1)} %gather_fusion), kind=kOutput, calls=%fused_computation.3 | convolution fusion | flops 536870912 | bytes 11010048 | tf_op jit(solution)/shard_map/tpml,tlo->tpmo/dot_general | solution.py:20
  35.3 0.0 copy-start.1
  35.3 9.2 %copy.12 = f32[8,8,128,256]{3,0,2,1:T(8,128)} copy(f32[8,8,128,256]{2,3,1,0:T(8,128)} %convolution_bitcast_fusion) | data formatting | bytes 16777216 | tf_op jit(solution)/shard_map/tpml,tlo->tpmo/dot_general | solution.py:20
  44.5 0.0 copy-done.1
  44.5 9.4 %convert_bitcast_fusion = bf16[8,8,128,256]{3,1,2,0:T(8,128)(2,1)S(1)} fusion(f32[8,8,128,256]{3,0,2,1:T(8,128)} %copy.12, f32[8]{0:T(128)S(1)} %compare_convert_fusion, s32[8]{0:T(128)S(1)} %bitcast.37), kind=kOutput, calls=%fused_computation.2 | convolution fusion | flops 203423872 | bytes 12582976 | tf_op jit(solution)/shard_map/tb,tpmo->pbmo/dot_general | solution.py:24
  53.9 3.0 %copy.13 = bf16[8,8,128,256]{3,2,1,0:T(8,128)(2,1)} copy(bf16[8,8,128,256]{3,1,2,0:T(8,128)(2,1)S(1)} %convert_bitcast_fusion) | data formatting | bytes 8388608 | tf_op jit(solution)/shard_map/convert_element_type | solution.py:26
  56.9 5.0 %gather_fusion.1 = bf16[16,8,64,256]{3,2,1,0:T(8,128)(2,1)} fusion(bf16[8,16,64,256]{3,2,1,0:T(8,128)(2,1)} %bitcast.33, s32[1024]{0:T(1024)S(1)} %pad_clamp_fusion), kind=kCustom, calls=%fused_computation.1 | custom fusion | bytes 8388672 | tf_op jit(solution)/shard_map/gather | solution.py:27
  61.9 2.5 %copy.14 = bf16[8,16,64,256]{3,2,1,0:T(8,128)(2,1)S(1)} copy(bf16[8,16,64,256]{3,2,0,1:T(8,128)(2,1)} %bitcast.34) | data formatting | bytes 8388608 | tf_op jit(solution)/shard_map/gather | solution.py:27
  64.4 6.1 %convolution_bitcast_fusion.1 = f32[1024,1024]{1,0:T(8,128)} fusion(bf16[8,1024,256]{2,1,0:T(8,128)(2,1)S(1)} %bitcast.35), kind=kOutput, calls=%fused_computation.4 | convolution fusion | flops 4294967296 | bytes 8388608 | tf_op jit(solution)/shard_map/prk,psk->rs/dot_general | solution.py:32
  70.5 0.0 reduce-scatter.2.cloned.1.call-update
  70.5 72.3 %reduce-scatter.2.cloned.1.call-done = f32[64,1024]{1,0:T(8,128)} async-done(((f32[1024,1024]{1,0:T(8,128)}), f32[64,1024]{1,0:T(8,128)}) %reduce-scatter.2.cloned.1.call-update) | async-done | bytes 262160 | tf_op jit(solution)/shard_map/reduce_scatter | solution.py:31
  142.8 1.7 %broadcast_multiply_fusion = f32[64,1024]{1,0:T(8,128)} fusion(f32[64,1024]{1,0:T(8,128)} %reduce-scatter.2.cloned.1.call-done), kind=kLoop, calls=%fused_computation.7 | loop fusion | flops 65536 | bytes 524288 | tf_op jit(solution)/shard_map/mul | solution.py:37
  (3 shorter events, 0.0 us)
Async XLA Ops:
  6.5 24.2 %copy-start = (bf16[1,8,8,128,128]{4,3,2,1,0:T(8,128)(2,1)S(1)}, bf16[1,8,8,128,128]{4,3,2,1,0:T(8,128)(2,1)}, u32[]{:S(2)}) copy-start(bf16[1,8,8,128,128]{4,3,2,1,0:T(8,128)(2,1)} %param.6) | copy-start | bytes 6291460
  8.3 21.9 %all-to-all-start = ((bf16[16,64,256]{2,1,0:T(8,128)(2,1)}), bf16[16,64,256]{2,1,0:T(8,128)(2,1)S(1)}, u32[]{:S(2)}, u32[]{:S(2)}) async-start(bf16[16,64,256]{2,1,0:T(8,128)(2,1)} %stack.2), calls=%async_computation | async-start | bytes 1048576 | tf_op jit(solution)/shard_map/all_to_all | solution.py:10
  15.7 127.1 %reduce-scatter.2.cloned.1.call-start = ((), (), s32[]{:S(2)}) async-start(), calls=%async_computation.2 | async-start | bytes 4456448 | tf_op jit(solution)/shard_map/reduce_scatter | solution.py:31
  35.3 9.2 %copy-start.1 = (s32[1,8]{1,0:T(1,128)S(1)}, s32[1,8]{1,0:T(1,128)}, u32[]{:S(2)}) copy-start(s32[1,8]{1,0:T(1,128)} %param.7) | copy-start | bytes 100
Sparse Core Ops, SparseCore 0:
  70.6 72.1 reduce-scatter.1
